TPU v7x, 32 devices: a whole 2x2x4 slice. The times are simulated.
32 devices in a mesh: lat: 8 (over z, y), tok: 4 (over x, core).
Axes of the slice: x: 2, y: 2, z: 4, core: 2. Of those that a mesh axis runs over, the one named last changes fastest.
Arguments:
- resid: bfloat16 [8192, 512], P('lat', 'tok'), may hold values from -6 to 6
- active_ids: int32 [512, 64], P('tok'), may hold values from 0 to 16383, all different within a row
- w_enc: bfloat16 [16384, 8192], P('lat', 'tok'), may hold values from -0.5 to 0.5
- w_dec: bfloat16 [16384, 8192], P('lat', 'tok'), may hold values from -0.0625 to 0.0625
- b_enc: float32 [16384], P('lat'), may hold values from -8 to 8
- b_dec: bfloat16 [8192], P('lat'), may hold values from -3 to 3
Outputs:
- grad_w_enc: bfloat16 [16384, 8192], P('lat', 'tok')
- grad_w_dec: bfloat16 [16384, 8192], P('lat', 'tok')
- grad_b_enc: float32 [16384], P('lat')
- grad_b_dec: float32 [8192], P('tok')
Inputs may be any that keep to these rules, and one draw needn't show every extreme that they name: `active_ids`: the 64 latents of a token are distinct, and every latent is active for some token.
All inputs are finite; a program needn't handle non-finite values.
Results may differ from a plain program's by a relative error of at most 0.0068.
Values may be sent and summed in bfloat16 or wider, within the bound.
A program may use at most 256 MiB of HBM per device.

v0:
```python
import jax
import jax.numpy as jnp
from jax import lax
from jax.sharding import PartitionSpec as P

f32 = jnp.float32
bf16 = jnp.bfloat16


def active_rows(ids, base, rows):
    word = 32 if rows % 32 == 0 else rows
    local = ids - base
    which = local // word
    place = local - which * word
    bit = lax.shift_left(jnp.int32(1), place)
    words = lax.iota(jnp.int32, rows // word)
    held = jnp.where(which[None, :, :] == words[:, None, None], bit[None, :, :], 0)
    held = jnp.sum(held, axis=1)
    shifts = lax.iota(jnp.int32, word)
    flags = (
        lax.shift_right_logical(
            held[:, None, :],
            jnp.broadcast_to(shifts[None, :, None], (rows // word, word, held.shape[1])),
        )
        & 1
    )
    return flags.reshape(rows, held.shape[1]).astype(f32)


def on_device(resid, active_ids, w_enc, w_dec, b_enc, b_dec):
    block_rows = w_enc.shape[0]
    width = w_enc.shape[1]
    lat_pos = lax.axis_index("lat")
    tok_pos = lax.axis_index("tok")
    tok_count = lax.axis_size("tok")
    lat_count = lax.axis_size("lat")
    rows = block_rows // tok_count
    feats = width // lat_count
    ids_all = lax.all_gather(active_ids, "tok", axis=0, tiled=True).T
    bias_full = lax.all_gather(b_dec, "lat", axis=0, tiled=True)
    resid_full = lax.all_gather(resid, "lat", axis=0, tiled=True)
    resid_mine = lax.all_to_all(resid_full, "tok", split_axis=0, concat_axis=1, tiled=True)
    bias_mine = lax.dynamic_slice_in_dim(bias_full, tok_pos * width, width, 0)
    centred = (resid_mine.astype(f32) - bias_mine.astype(f32)[:, None]).astype(bf16)
    active = active_rows(ids_all, lat_pos * block_rows + tok_pos * rows, rows)
    b_rows = lax.dynamic_slice_in_dim(b_enc, tok_pos * rows, rows, 0)
    pre_part = jnp.dot(w_enc, centred, preferred_element_type=f32).astype(bf16)
    pre = lax.psum_scatter(pre_part, "tok", scatter_dimension=0, tiled=True)
    codes_rows = ((pre.astype(f32) + b_rows[:, None]) * active).astype(bf16)
    codes = lax.all_gather(codes_rows, "tok", axis=0, tiled=True)
    recon_part = lax.dot_general(
        w_dec, codes, (((0,), (0,)), ((), ())), preferred_element_type=f32
    ).astype(bf16)
    recon = lax.psum_scatter(recon_part, "lat", scatter_dimension=0, tiled=True)
    r_rows = lax.dynamic_slice_in_dim(resid_mine, lat_pos * feats, feats, 0)
    bd_rows = lax.dynamic_slice_in_dim(bias_mine, lat_pos * feats, feats, 0)
    error_rows = (recon.astype(f32) + bd_rows.astype(f32)[:, None] - r_rows.astype(f32)).astype(
        bf16
    )
    errors = lax.all_gather(error_rows, "lat", axis=0, tiled=True)
    gc_part = jnp.dot(w_dec, errors, preferred_element_type=f32).astype(bf16)
    gc = lax.psum_scatter(gc_part, "tok", scatter_dimension=0, tiled=True)
    gp_rows = (gc.astype(f32) * active).astype(bf16)
    grad_pre = lax.all_gather(gp_rows, "tok", axis=0, tiled=True)
    grad_w_dec = lax.dot_general(
        codes, errors, (((1,), (1,)), ((), ())), preferred_element_type=f32
    ).astype(bf16)
    grad_b_enc = jnp.sum(grad_pre.astype(f32), axis=1)
    high = grad_b_enc.astype(bf16)
    rest = grad_b_enc - high.astype(f32)
    mid = rest.astype(bf16)
    low = (rest - mid.astype(f32)).astype(bf16)
    parts = jnp.stack([high, mid, low])
    back = jnp.sum(jnp.dot(parts, w_enc, preferred_element_type=f32), axis=0)
    back = lax.psum(back, "lat")
    error_total = jnp.sum(errors.astype(f32), axis=1)
    grad_w_enc = lax.dot_general(
        grad_pre, centred, (((1,), (1,)), ((), ())), preferred_element_type=f32
    ).astype(bf16)
    return (grad_w_enc, grad_w_dec, grad_b_enc, error_total - back)


def solution(mesh):
    return jax.shard_map(
        on_device,
        mesh=mesh,
        in_specs=(
            P("lat", "tok"),
            P("tok", None),
            P("lat", "tok"),
            P("lat", "tok"),
            P("lat"),
            P("lat"),
        ),
        out_specs=(P("lat", "tok"), P("lat", "tok"), P("lat"), P("tok")),
        check_vma=False,
    )
```

profile of v0, /device:TPU:0, one launch (start us, length us, event | category | flops | bytes accessed | tf_op | source)
XLA Modules:
  0.0 399.6 jit_solution(10416619332048094439)
XLA Ops:
  7.9 54.2 %all-gather.5.cloned.1.call-done = bf16[8192,128]{1,0:T(8,128)(2,1)} async-done(((bf16[1024,128]{1,0:T(8,128)(2,1)}), bf16[8192,128]{1,0:T(8,128)(2,1)}) %all-gather.5.cloned.1.call-update) | async-done | bytes 2097168 | tf_op jit(solution)/shard_map/all_gather | solution.py:41
  62.1 3.9 copy.15
  66.1 3.7 all-to-all-start
  69.9 26.0 %all_gather.19 = bf16[8192]{0:T(1024)(128)(2,1)S(1)} all-gather(bf16[1024]{0:T(1024)(128)(2,1)S(1)} %copy-done.5), channel_id=1, replica_groups=mesh['lat'=8,'tok'=4] {'lat'}, dimensions={0}, use_global_device_ids=true | all-gather | bytes 18432 | tf_op jit(solution)/shard_map/all_gather | solution.py:40
  95.9 9.9 %fusion = bf16[2048,512]{0,1:T(8,128)(2,1)} fusion(bf16[2048,2048]{1,0:T(8,128)(2,1)} %param.8, bf16[2048,512]{0,1:T(8,128)(2,1)S(1)} %bitcast.43, f32[2048]{0:T(1024)S(1)} %dynamic-slice_convert_fusion), kind=kOutput, calls=%fused_computation.8 | convolution fusion | flops 4299161600 | bytes 12591104 | tf_op jit(solution)/shard_map/dot_general | solution.py:47
  106.5 5.5 %all_gather.20 = s32[512,64]{0,1:T(8,128)S(1)} all-gather(s32[128,64]{0,1:T(8,128)S(1)} %copy-done.4), channel_id=1, replica_groups=mesh['lat'=8,'tok'=4] {'tok'}, dimensions={0}, use_global_device_ids=true | all-gather | bytes 163840 | tf_op jit(solution)/shard_map/all_gather | solution.py:39
  112.8 0.8 dynamic_slice.15
  113.6 21.5 %reduce-scatter.4.cloned.1.call-done = bf16[512,512]{0,1:T(8,128)(2,1)} async-done(((bf16[2048,512]{0,1:T(8,128)(2,1)}), bf16[512,512]{0,1:T(8,128)(2,1)}) %reduce-scatter.4.cloned.1.call-update) | async-done | bytes 524304 | tf_op jit(solution)/shard_map/reduce_scatter | solution.py:48
  135.1 2.1 multiply_convert_fusion.1
  137.2 22.7 %all-gather.7.cloned.1.call-done = bf16[2048,512]{0,1:T(8,128)(2,1)} async-done(((bf16[512,512]{0,1:T(8,128)(2,1)}), bf16[2048,512]{0,1:T(8,128)(2,1)}) %all-gather.7.cloned.1.call-update) | async-done | bytes 2097168 | tf_op jit(solution)/shard_map/all_gather | solution.py:50
  159.9 9.8 %fusion.1 = bf16[2048,512]{0,1:T(8,128)(2,1)} fusion(bf16[2048,512]{0,1:T(8,128)(2,1)} %all-gather.7.cloned.1.call-done, bf16[2048,2048]{1,0:T(8,128)(2,1)} %param.9), kind=kOutput, calls=%fused_computation.9 | convolution fusion | flops 4296015872 | bytes 12582912 | tf_op jit(solution)/shard_map/dot_general | solution.py:51
  169.9 68.3 %reduce-scatter.6.cloned.1.call-done = bf16[256,512]{0,1:T(8,128)(2,1)} async-done(((bf16[2048,512]{0,1:T(8,128)(2,1)}), bf16[256,512]{0,1:T(8,128)(2,1)}) %reduce-scatter.6.cloned.1.call-update) | async-done | bytes 262160 | tf_op jit(solution)/shard_map/reduce_scatter | solution.py:54
  238.2 1.7 subtract_convert_fusion.3
  240.1 51.0 %all-gather.9.cloned.1.call-done = bf16[2048,512]{0,1:T(8,128)(2,1)} async-done(((bf16[256,512]{0,1:T(8,128)(2,1)}), bf16[2048,512]{0,1:T(8,128)(2,1)}) %all-gather.9.cloned.1.call-update) | async-done | bytes 2097168 | tf_op jit(solution)/shard_map/all_gather | solution.py:60
  291.1 9.9 %fusion.2 = bf16[2048,512]{0,1:T(8,128)(2,1)} fusion(bf16[2048,512]{0,1:T(8,128)(2,1)} %all-gather.9.cloned.1.call-done, bf16[2048,2048]{1,0:T(8,128)(2,1)} %param.9), kind=kOutput, calls=%fused_computation.10 | convolution fusion | flops 4296015872 | bytes 12582912 | tf_op jit(solution)/shard_map/dot_general | solution.py:61
  301.2 29.5 %reduce-scatter.8.cloned.1.call-done = bf16[512,512]{0,1:T(8,128)(2,1)} async-done(((bf16[2048,512]{0,1:T(8,128)(2,1)}), bf16[512,512]{0,1:T(8,128)(2,1)}) %reduce-scatter.8.cloned.1.call-update) | async-done | bytes 524304 | tf_op jit(solution)/shard_map/reduce_scatter | solution.py:62
  330.7 2.0 multiply_convert_fusion
  332.8 2.1 convert_reduce_fusion
  335.0 8.4 %convolution_convert_fusion = bf16[2048,2048]{1,0:T(8,128)(2,1)} fusion(bf16[2048,512]{0,1:T(8,128)(2,1)} %all-gather.7.cloned.1.call-done, bf16[2048,512]{0,1:T(8,128)(2,1)S(1)} %copy-done.2), kind=kOutput, calls=%fused_computation | convolution fusion | flops 4299161600 | bytes 12582912 | tf_op jit(solution)/shard_map/dot_general | solution.py:65
  343.4 12.2 %all-gather.11.cloned.1.call-done = bf16[2048,512]{0,1:T(8,128)(2,1)} async-done(((bf16[512,512]{0,1:T(8,128)(2,1)}), bf16[2048,512]{0,1:T(8,128)(2,1)}) %all-gather.11.cloned.1.call-update) | async-done | bytes 2097168 | tf_op jit(solution)/shard_map/all_gather | solution.py:64
  355.5 2.0 convert_reduce_fusion.1
  357.5 4.6 %convolution_reduce_fusion = f32[2048]{0:T(1024)S(1)} fusion(bf16[2048,2048]{1,0:T(8,128)(2,1)} %param.8, bf16[1,2048]{1,0:T(2,128)(2,1)S(1)} %get-tuple-element.7, bf16[1,2048]{1,0:T(2,128)(2,1)S(1)} %get-tuple-element.6, bf16[1,2048]{1,0:T(2,128)(2,1)S(1)} %convert_element_type.154), kind=kOutput, calls=%fused_computation.13 | convolution fusion | flops 25206784 | bytes 8409088 | tf_op jit(solution)/shard_map/dot_general | solution.py:74
  362.1 21.6 %psum.7 = f32[2048]{0:T(1024)S(1)} all-reduce(f32[2048]{0:T(1024)S(1)} %convolution_reduce_fusion), channel_id=1, replica_groups=mesh['lat'=8,'tok'=4] {'lat'}, use_global_device_ids=true, to_apply=%region_7.8 | all-reduce | flops 2048 | bytes 16384 | tf_op jit(solution)/shard_map/psum | solution.py:75
  384.4 8.4 %convolution_convert_fusion.1 = bf16[2048,2048]{1,0:T(8,128)(2,1)} fusion(bf16[2048,512]{0,1:T(8,128)(2,1)} %all-gather.11.cloned.1.call-done, bf16[2048,512]{0,1:T(8,128)(2,1)S(1)} %bitcast.45, f32[2048]{0:T(1024)S(1)} %dynamic-slice_convert_fusion), kind=kOutput, calls=%fused_computation.1 | convolution fusion | flops 4302307328 | bytes 12591104 | tf_op jit(solution)/shard_map/dot_general | solution.py:77
  (38 shorter events, 3.6 us)
Async XLA Ops:
  7.2 55.0 %all-gather.5.cloned.1.call-start = ((), (), s32[]{:S(2)}) async-start(), calls=%async_computation.4 | async-start | bytes 2359296 | tf_op jit(solution)/shard_map/all_gather | solution.py:41
  66.1 3.8 copy-start.5
  66.1 29.8 %all-to-all-start = ((bf16[4,2048,128]{1,2,0:T(8,128)(2,1)}), bf16[4,2048,128]{1,2,0:T(8,128)(2,1)S(1)}, u32[]{:S(2)}, u32[]{:S(2)}) async-start(bf16[4,2048,128]{1,2,0:T(8,128)(2,1)} %copy.15), calls=%async_computation | async-start | bytes 4194304 | tf_op jit(solution)/shard_map/all_to_all | solution.py:42
  69.8 65.3 %reduce-scatter.4.cloned.1.call-start = ((), (), s32[]{:S(2)}) async-start(), calls=%async_computation.5 | async-start | bytes 2621440 | tf_op jit(solution)/shard_map/reduce_scatter | solution.py:48
  95.9 9.9 %copy-start = (bf16[4,2048,128]{1,2,0:T(8,128)(2,1)}, bf16[4,2048,128]{1,2,0:T(8,128)(2,1)S(1)}, u32[]{:S(2)}) copy-start(bf16[4,2048,128]{1,2,0:T(8,128)(2,1)S(1)} %all-to-all-done) | copy-start | bytes 6291460
  105.8 0.8 copy-start.4
  105.8 54.1 %all-gather.7.cloned.1.call-start = ((), (), s32[]{:S(2)}) async-start(), calls=%async_computation.6 | async-start | bytes 2621440 | tf_op jit(solution)/shard_map/all_gather | solution.py:50
  137.2 101.1 %reduce-scatter.6.cloned.1.call-start = ((), (), s32[]{:S(2)}) async-start(), calls=%async_computation.7 | async-start | bytes 2359296 | tf_op jit(solution)/shard_map/reduce_scatter | solution.py:54
  169.8 68.5 %copy-start.1 = (bf16[4,2048,128]{1,2,0:T(8,128)(2,1)S(1)}, bf16[4,2048,128]{1,2,0:T(8,128)(2,1)}, u32[]{:S(2)}) copy-start(bf16[4,2048,128]{1,2,0:T(8,128)(2,1)} %copy-done) | copy-start | bytes 6291460
  169.8 121.3 %all-gather.9.cloned.1.call-start = ((), (), s32[]{:S(2)}) async-start(), calls=%async_computation.8 | async-start | bytes 2359296 | tf_op jit(solution)/shard_map/all_gather | solution.py:60
  240.0 90.7 %reduce-scatter.8.cloned.1.call-start = ((), (), s32[]{:S(2)}) async-start(), calls=%async_computation.9 | async-start | bytes 2621440 | tf_op jit(solution)/shard_map/reduce_scatter | solution.py:62
  301.0 54.6 %all-gather.11.cloned.1.call-start = ((), (), s32[]{:S(2)}) async-start(), calls=%async_computation.10 | async-start | bytes 2621440 | tf_op jit(solution)/shard_map/all_gather | solution.py:64
  332.8 2.2 copy-start.2
  357.5 4.6 %copy-start.3 = (f32[2048]{0:T(1024)}, f32[2048]{0:T(1024)S(1)}, u32[]{:S(2)}) copy-start(f32[2048]{0:T(1024)S(1)} %convert_reduce_fusion.1) | copy-start | bytes 24580
Sparse Core Ops, SparseCore 0:
  10.1 51.9 all-gather.4
  105.9 29.1 reduce-scatter.3
  137.3 22.5 all-gather.6
  169.9 68.2 reduce-scatter.5
  240.9 50.1 all-gather.8
  301.1 29.5 reduce-scatter.7
  332.9 22.5 all-gather.10
where the time goes:
time: 400 us
  waiting for transfers between devices  260 us (65%)
  blocking collectives  53.1 us (13%)
  matrix products  50.9 us (13%)
  between operations  14.3 us (4%)
  other arithmetic  11 us (3%)
  local copies, waits for them, and re-layouts  5.95 us (1%)
  starting transfers between devices  4.21 us (1%)
    reduce_scatter x1, waiting for transfers between devices, on_device(): recon = lax.psum_scatter(recon_part, 'lat', scatter_dimension=0, tiled=True)  68.3 us
    all_gather x1, waiting for transfers between devices, on_device(): resid_full = lax.all_gather(resid, 'lat', axis=0, tiled=True)  54.2 us
    all_gather x1, waiting for transfers between devices, on_device(): errors = lax.all_gather(error_rows, 'lat', axis=0, tiled=True)  51 us
    reduce_scatter x1, waiting for transfers between devices, on_device(): gc = lax.psum_scatter(gc_part, 'tok', scatter_dimension=0, tiled=True)  29.5 us
    all_gather x1, blocking collectives, on_device(): bias_full = lax.all_gather(b_dec, 'lat', axis=0, tiled=True)  26 us
    all_gather x1, waiting for transfers between devices, on_device(): codes = lax.all_gather(codes_rows, 'tok', axis=0, tiled=True)  22.7 us
    psum x1, blocking collectives, on_device(): back = lax.psum(back, 'lat')  21.6 us
    reduce_scatter x1, waiting for transfers between devices, on_device(): pre = lax.psum_scatter(pre_part, 'tok', scatter_dimension=0, tiled=True)  21.5 us
  transfers between devices with their start and end apart: 8, of which 7 were waited for; matrix products, arithmetic and copies ran while one was open for 3% of the time, Pallas kernels for 0%

commit v1 on v0

--- a/solution.py
+++ b/solution.py
@@ -38,7 +38,15 @@
     feats = width // lat_count
     ids_all = lax.all_gather(active_ids, "tok", axis=0, tiled=True).T
     bias_full = lax.all_gather(b_dec, "lat", axis=0, tiled=True)
-    resid_full = lax.all_gather(resid, "lat", axis=0, tiled=True)
+    ways, here = (lax.axis_size("lat"), lax.axis_index("lat"))
+    grown, reach = (resid, 1)
+    while reach < ways:
+        theirs = lax.ppermute(grown, "lat", [(d, d ^ reach) for d in range(ways)])
+        mine_first = jnp.concatenate([grown, theirs], axis=0)
+        theirs_first = jnp.concatenate([theirs, grown], axis=0)
+        grown = jnp.where(here & reach == 0, mine_first, theirs_first)
+        reach = 2 * reach
+    resid_full = grown
     resid_mine = lax.all_to_all(resid_full, "tok", split_axis=0, concat_axis=1, tiled=True)
     bias_mine = lax.dynamic_slice_in_dim(bias_full, tok_pos * width, width, 0)
     centred = (resid_mine.astype(f32) - bias_mine.astype(f32)[:, None]).astype(bf16)

time: 400 us -> 419 us (1.048)
  waiting for transfers between devices: 260 us -> 270 us
  starting transfers between devices: 4.21 us -> 11.6 us
    ppermute x0 -> x3, waiting for transfers between devices: none -> 62.2 us  [on_device(): theirs = lax.ppermute(grown, 'lat', [(d, d ^ reach) for d in range(ways)])]
    all_gather x1 -> x0, waiting for transfers between devices: 54.2 us -> none  [on_device(): resid_full = lax.all_gather(resid, 'lat', axis=0, tiled=True)]
    ppermute x0 -> x3, starting transfers between devices: none -> 7.45 us  [on_device(): theirs = lax.ppermute(grown, 'lat', [(d, d ^ reach) for d in range(ways)])]
  transfers between devices with their start and end apart: 8 -> 10, of which waited for: 7 -> 9; matrix products, arithmetic and copies ran while one was open for 3% -> 3% of each run, Pallas kernels for 0% -> 0%
where the time goes in v1:
time: 419 us
  waiting for transfers between devices  270 us (64%)
  blocking collectives  53.1 us (13%)
  matrix products  50.9 us (12%)
  other arithmetic  14.5 us (3%)
  between operations  14.3 us (3%)
  starting transfers between devices  11.6 us (3%)
  local copies, waits for them, and re-layouts  4.61 us (1%)
    reduce_scatter x1, waiting for transfers between devices, on_device(): recon = lax.psum_scatter(recon_part, 'lat', scatter_dimension=0, tiled=True)  68.3 us
    ppermute x3, waiting for transfers between devices, on_device(): theirs = lax.ppermute(grown, 'lat', [(d, d ^ reach) for d in range(ways)])  62.2 us
    all_gather x1, waiting for transfers between devices, on_device(): errors = lax.all_gather(error_rows, 'lat', axis=0, tiled=True)  50.9 us
    reduce_scatter x1, waiting for transfers between devices, on_device(): gc = lax.psum_scatter(gc_part, 'tok', scatter_dimension=0, tiled=True)  29.7 us
    all_gather x1, blocking collectives, on_device(): bias_full = lax.all_gather(b_dec, 'lat', axis=0, tiled=True)  26 us
    reduce_scatter x1, waiting for transfers between devices, on_device(): pre = lax.psum_scatter(pre_part, 'tok', scatter_dimension=0, tiled=True)  23.5 us
    all_gather x1, waiting for transfers between devices, on_device(): codes = lax.all_gather(codes_rows, 'tok', axis=0, tiled=True)  22.7 us
    psum x1, blocking collectives, on_device(): back = lax.psum(back, 'lat')  21.6 us
  transfers between devices with their start and end apart: 10, of which 9 were waited for; matrix products, arithmetic and copies ran while one was open for 3% of the time, Pallas kernels for 0%

profile of v1, /device:TPU:0, one launch (start us, length us, event | category | flops | bytes accessed | tf_op | source)
XLA Modules:
  0.0 418.5 jit_solution(8640735733563791027)
XLA Ops:
  7.2 3.0 collective-permute-start
  10.2 6.5 %collective-permute-done = bf16[1024,128]{1,0:T(8,128)(2,1)S(1)} collective-permute-done((bf16[1024,128]{1,0:T(8,128)(2,1)}, bf16[1024,128]{1,0:T(8,128)(2,1)S(1)}, u32[]{:S(2)}, u32[]{:S(2)}) %collective-permute-start) | collective-permute-done | bytes 262176 | tf_op jit(solution)/shard_map/ppermute | solution.py:44
  19.7 11.3 %collective-permute-done.1 = bf16[2048,128]{1,0:T(8,128)(2,1)S(1)} collective-permute-done((bf16[2048,128]{1,0:T(8,128)(2,1)S(1)}, bf16[2048,128]{1,0:T(8,128)(2,1)S(1)}, u32[]{:S(2)}, u32[]{:S(2)}) %collective-permute-start.1) | collective-permute-done | bytes 524320 | tf_op jit(solution)/shard_map/ppermute | solution.py:44
  31.3 2.6 collective-permute-start.2
  33.9 44.4 %collective-permute-done.2 = bf16[4096,128]{1,0:T(8,128)(2,1)} collective-permute-done((bf16[4096,128]{1,0:T(8,128)(2,1)S(1)}, bf16[4096,128]{1,0:T(8,128)(2,1)}, u32[]{:S(2)}, u32[]{:S(2)}) %collective-permute-start.2) | collective-permute-done | bytes 1048608 | tf_op jit(solution)/shard_map/ppermute | solution.py:44
  78.3 2.1 maximum_select_fusion
  80.4 2.6 copy.15
  83.0 3.7 all-to-all-start
  86.8 26.0 %all_gather.15 = bf16[8192]{0:T(1024)(128)(2,1)S(1)} all-gather(bf16[1024]{0:T(1024)(128)(2,1)S(1)} %copy-done.5), channel_id=1, replica_groups=mesh['lat'=8,'tok'=4] {'lat'}, dimensions={0}, use_global_device_ids=true | all-gather | bytes 18432 | tf_op jit(solution)/shard_map/all_gather | solution.py:40
  112.8 9.9 %fusion = bf16[2048,512]{0,1:T(8,128)(2,1)} fusion(bf16[2048,2048]{1,0:T(8,128)(2,1)} %param.8, bf16[2048,512]{0,1:T(8,128)(2,1)S(1)} %bitcast.44, f32[2048]{0:T(1024)S(1)} %dynamic-slice_convert_fusion), kind=kOutput, calls=%fused_computation.8 | convolution fusion | flops 4299161600 | bytes 12591104 | tf_op jit(solution)/shard_map/dot_general | solution.py:55
  123.5 5.4 %all_gather.16 = s32[512,64]{0,1:T(8,128)S(1)} all-gather(s32[128,64]{0,1:T(8,128)S(1)} %copy-done.4), channel_id=1, replica_groups=mesh['lat'=8,'tok'=4] {'tok'}, dimensions={0}, use_global_device_ids=true | all-gather | bytes 163840 | tf_op jit(solution)/shard_map/all_gather | solution.py:39
  130.5 23.5 %reduce-scatter.4.cloned.1.call-done = bf16[512,512]{0,1:T(8,128)(2,1)} async-done(((bf16[2048,512]{0,1:T(8,128)(2,1)}), bf16[512,512]{0,1:T(8,128)(2,1)}) %reduce-scatter.4.cloned.1.call-update) | async-done | bytes 524304 | tf_op jit(solution)/shard_map/reduce_scatter | solution.py:56
  156.1 22.7 %all-gather.4.cloned.1.call-done = bf16[2048,512]{0,1:T(8,128)(2,1)} async-done(((bf16[512,512]{0,1:T(8,128)(2,1)}), bf16[2048,512]{0,1:T(8,128)(2,1)}) %all-gather.4.cloned.1.call-update) | async-done | bytes 2097168 | tf_op jit(solution)/shard_map/all_gather | solution.py:58
  178.8 9.8 %fusion.1 = bf16[2048,512]{0,1:T(8,128)(2,1)} fusion(bf16[2048,512]{0,1:T(8,128)(2,1)} %all-gather.4.cloned.1.call-done, bf16[2048,2048]{1,0:T(8,128)(2,1)} %param.9), kind=kOutput, calls=%fused_computation.9 | convolution fusion | flops 4296015872 | bytes 12582912 | tf_op jit(solution)/shard_map/dot_general | solution.py:59
  188.8 68.3 %reduce-scatter.6.cloned.1.call-done = bf16[256,512]{0,1:T(8,128)(2,1)} async-done(((bf16[2048,512]{0,1:T(8,128)(2,1)}), bf16[256,512]{0,1:T(8,128)(2,1)}) %reduce-scatter.6.cloned.1.call-update) | async-done | bytes 262160 | tf_op jit(solution)/shard_map/reduce_scatter | solution.py:62
  259.1 50.9 %all-gather.6.cloned.1.call-done = bf16[2048,512]{0,1:T(8,128)(2,1)} async-done(((bf16[256,512]{0,1:T(8,128)(2,1)}), bf16[2048,512]{0,1:T(8,128)(2,1)}) %all-gather.6.cloned.1.call-update) | async-done | bytes 2097168 | tf_op jit(solution)/shard_map/all_gather | solution.py:68
  310.0 9.9 %fusion.2 = bf16[2048,512]{0,1:T(8,128)(2,1)} fusion(bf16[2048,512]{0,1:T(8,128)(2,1)} %all-gather.6.cloned.1.call-done, bf16[2048,2048]{1,0:T(8,128)(2,1)} %param.9), kind=kOutput, calls=%fused_computation.10 | convolution fusion | flops 4296015872 | bytes 12582912 | tf_op jit(solution)/shard_map/dot_general | solution.py:69
  319.9 29.7 %reduce-scatter.8.cloned.1.call-done = bf16[512,512]{0,1:T(8,128)(2,1)} async-done(((bf16[2048,512]{0,1:T(8,128)(2,1)}), bf16[512,512]{0,1:T(8,128)(2,1)}) %reduce-scatter.8.cloned.1.call-update) | async-done | bytes 524304 | tf_op jit(solution)/shard_map/reduce_scatter | solution.py:70
  351.7 2.1 convert_reduce_fusion
  353.9 8.4 %convolution_convert_fusion = bf16[2048,2048]{1,0:T(8,128)(2,1)} fusion(bf16[2048,512]{0,1:T(8,128)(2,1)} %all-gather.4.cloned.1.call-done, bf16[2048,512]{0,1:T(8,128)(2,1)S(1)} %copy-done.2), kind=kOutput, calls=%fused_computation | convolution fusion | flops 4299161600 | bytes 12582912 | tf_op jit(solution)/shard_map/dot_general | solution.py:73
  362.3 12.2 %all-gather.8.cloned.1.call-done = bf16[2048,512]{0,1:T(8,128)(2,1)} async-done(((bf16[512,512]{0,1:T(8,128)(2,1)}), bf16[2048,512]{0,1:T(8,128)(2,1)}) %all-gather.8.cloned.1.call-update) | async-done | bytes 2097168 | tf_op jit(solution)/shard_map/all_gather | solution.py:72
  376.5 4.6 %convolution_reduce_fusion = f32[2048]{0:T(1024)S(1)} fusion(bf16[2048,2048]{1,0:T(8,128)(2,1)} %param.8, bf16[1,2048]{1,0:T(2,128)(2,1)S(1)} %get-tuple-element.7, bf16[1,2048]{1,0:T(2,128)(2,1)S(1)} %get-tuple-element.6, bf16[1,2048]{1,0:T(2,128)(2,1)S(1)} %convert_element_type.154), kind=kOutput, calls=%fused_computation.14 | convolution fusion | flops 25206784 | bytes 8409088 | tf_op jit(solution)/shard_map/dot_general | solution.py:82
  381.1 21.6 %psum.7 = f32[2048]{0:T(1024)S(1)} all-reduce(f32[2048]{0:T(1024)S(1)} %convolution_reduce_fusion), channel_id=1, replica_groups=mesh['lat'=8,'tok'=4] {'lat'}, use_global_device_ids=true, to_apply=%region_7.8 | all-reduce | flops 2048 | bytes 16384 | tf_op jit(solution)/shard_map/psum | solution.py:83
  403.3 8.4 %convolution_convert_fusion.1 = bf16[2048,2048]{1,0:T(8,128)(2,1)} fusion(bf16[2048,512]{0,1:T(8,128)(2,1)} %all-gather.8.cloned.1.call-done, bf16[2048,512]{0,1:T(8,128)(2,1)S(1)} %bitcast.46, f32[2048]{0:T(1024)S(1)} %dynamic-slice_convert_fusion), kind=kOutput, calls=%fused_computation.1 | convolution fusion | flops 4302307328 | bytes 12591104 | tf_op jit(solution)/shard_map/dot_general | solution.py:85
  (44 shorter events, 14.7 us)
Async XLA Ops:
  7.2 9.5 %collective-permute-start = (bf16[1024,128]{1,0:T(8,128)(2,1)}, bf16[1024,128]{1,0:T(8,128)(2,1)S(1)}, u32[]{:S(2)}, u32[]{:S(2)}) collective-permute-start(bf16[1024,128]{1,0:T(8,128)(2,1)} %param.6), channel_id=1, source_target_pairs={{0,4},{4,0},{8,12},{12,8},{16,20},{20,16},{24,28},{28,24},{1,5},{5... | collective-permute-start | bytes 786440 | tf_op jit(solution)/shard_map/ppermute | solution.py:44
  17.9 13.2 %collective-permute-start.1 = (bf16[2048,128]{1,0:T(8,128)(2,1)S(1)}, bf16[2048,128]{1,0:T(8,128)(2,1)S(1)}, u32[]{:S(2)}, u32[]{:S(2)}) collective-permute-start(bf16[2048,128]{1,0:T(8,128)(2,1)S(1)} %maximum_select_fusion.2), channel_id=1, source_target_pairs={{0,8},{4,12},{8,0},{12,4},{16,24},{20,28},{24,16},{28,20},{1,9},{5... | collective-permute-start | bytes 1572872 | tf_op jit(solution)/shard_map/ppermute | solution.py:44
  31.3 47.0 %collective-permute-start.2 = (bf16[4096,128]{1,0:T(8,128)(2,1)S(1)}, bf16[4096,128]{1,0:T(8,128)(2,1)}, u32[]{:S(2)}, u32[]{:S(2)}) collective-permute-start(bf16[4096,128]{1,0:T(8,128)(2,1)S(1)} %maximum_select_fusion.1), channel_id=1, source_target_pairs={{0,16},{4,20},{8,24},{12,28},{16,0},{20,4},{24,8},{28,12},{1,17},{... | collective-permute-start | bytes 3145736 | tf_op jit(solution)/shard_map/ppermute | solution.py:44
  83.0 3.8 copy-start.5
  83.0 29.8 %all-to-all-start = ((bf16[4,2048,128]{1,2,0:T(8,128)(2,1)}), bf16[4,2048,128]{1,2,0:T(8,128)(2,1)S(1)}, u32[]{:S(2)}, u32[]{:S(2)}) async-start(bf16[4,2048,128]{1,2,0:T(8,128)(2,1)} %copy.15), calls=%async_computation | async-start | bytes 4194304 | tf_op jit(solution)/shard_map/all_to_all | solution.py:50
  86.8 67.2 %reduce-scatter.4.cloned.1.call-start = ((), (), s32[]{:S(2)}) async-start(), calls=%async_computation.4 | async-start | bytes 2621440 | tf_op jit(solution)/shard_map/reduce_scatter | solution.py:56
  112.8 9.9 %copy-start = (bf16[4,2048,128]{1,2,0:T(8,128)(2,1)}, bf16[4,2048,128]{1,2,0:T(8,128)(2,1)S(1)}, u32[]{:S(2)}) copy-start(bf16[4,2048,128]{1,2,0:T(8,128)(2,1)S(1)} %all-to-all-done) | copy-start | bytes 6291460
  122.7 0.8 copy-start.4
  122.7 56.1 %all-gather.4.cloned.1.call-start = ((), (), s32[]{:S(2)}) async-start(), calls=%async_computation.5 | async-start | bytes 2621440 | tf_op jit(solution)/shard_map/all_gather | solution.py:58
  156.1 101.1 %reduce-scatter.6.cloned.1.call-start = ((), (), s32[]{:S(2)}) async-start(), calls=%async_computation.6 | async-start | bytes 2359296 | tf_op jit(solution)/shard_map/reduce_scatter | solution.py:62
  188.7 68.5 %copy-start.1 = (bf16[4,2048,128]{1,2,0:T(8,128)(2,1)S(1)}, bf16[4,2048,128]{1,2,0:T(8,128)(2,1)}, u32[]{:S(2)}) copy-start(bf16[4,2048,128]{1,2,0:T(8,128)(2,1)} %copy-done) | copy-start | bytes 6291460
  188.7 121.3 %all-gather.6.cloned.1.call-start = ((), (), s32[]{:S(2)}) async-start(), calls=%async_computation.7 | async-start | bytes 2359296 | tf_op jit(solution)/shard_map/all_gather | solution.py:68
  258.9 90.8 %reduce-scatter.8.cloned.1.call-start = ((), (), s32[]{:S(2)}) async-start(), calls=%async_computation.8 | async-start | bytes 2621440 | tf_op jit(solution)/shard_map/reduce_scatter | solution.py:70
  319.9 54.6 %all-gather.8.cloned.1.call-start = ((), (), s32[]{:S(2)}) async-start(), calls=%async_computation.9 | async-start | bytes 2621440 | tf_op jit(solution)/shard_map/all_gather | solution.py:72
  351.7 2.2 copy-start.2
  376.4 4.6 %copy-start.3 = (f32[2048]{0:T(1024)}, f32[2048]{0:T(1024)S(1)}, u32[]{:S(2)}) copy-start(f32[2048]{0:T(1024)S(1)} %convert_reduce_fusion.1) | copy-start | bytes 24580
Sparse Core Ops, SparseCore 0:
  122.8 31.1 reduce-scatter.3
  156.2 22.5 all-gather.3
  188.8 68.2 reduce-scatter.5
  259.8 50.1 all-gather.5
  320.0 29.6 reduce-scatter.7
  351.8 22.5 all-gather.7
